TPU v7x, 256 devices: a whole 4x4x8 slice. The times are simulated.
256 devices in a mesh: head: 16 (over z, x_lo), blk: 16 (over x_hi, y, core).
Axes of the slice: x: 4 (x_hi: 2, x_lo: 2; x = x_hi * 2 + x_lo), y: 4, z: 8, core: 2. Of those that a mesh axis runs over, the one named last changes fastest.
Arguments:
- queries: bfloat16 [2, 16384, 2048], P(None, ('head', 'blk')), may hold values from -320 to 320
- key_codes: bfloat16 [2, 16384, 2048], P(None, ('head', 'blk')), may hold values from -6 to 6
- key_scales: bfloat16 [2, 16384, 16], P(None, ('head', 'blk')), may hold values from 0.5 to 2
- value_codes: bfloat16 [2, 16384, 2048], P(None, ('head', 'blk')), may hold values from -6 to 6
- value_scales: bfloat16 [2, 16384, 16], P(None, ('head', 'blk')), may hold values from 0.5 to 2
- doc_lengths: int32 [2, 8], replicated, may hold values from 1 to 8192, 16384 in all within a row
Outputs:
- attended: bfloat16 [2, 16384, 2048], P(None, ('head', 'blk'))
All inputs are finite; a program needn't handle non-finite values.
Results may differ from a plain program's by a relative error of at most 0.0055.
The roundings to bfloat16 on the way count: a program that leaves them out, or rounds other values in their place, can miss the bound.
Values may be sent and summed in bfloat16 or wider, within the bound.
A program may use at most 128 MiB of HBM per device.

v0:
```python
import functools
import math

import jax
import jax.numpy as jnp
from jax import lax
from jax.experimental import pallas as pl
from jax.experimental.pallas import tpu as pltpu
from jax.sharding import PartitionSpec as P

MESH = pl.DeviceIdType.MESH
NEG = -1e30
LEAST = -(1 << 31)
VMEM_ASK = 60 * 1024 * 1024
HD = 128
XH, XL, CORES = 2, 2, 2


def hadamard_matrix():
    both = lax.broadcasted_iota(jnp.int32, (HD, HD), 0) & lax.broadcasted_iota(jnp.int32, (HD, HD), 1)
    parity = jnp.zeros((HD, HD), jnp.int32)
    for shift in range(7):
        parity = parity + ((both >> shift) & 1)
    return (1 - 2 * (parity & 1)).astype(jnp.float32).astype(jnp.bfloat16)


def kernel(heads, blocks, doc_ref, q_hbm, kc_hbm, ks_ref, vc_hbm, vs_ref, out_hbm,
           codes, wide, stage, kv, qv, ov, s_a, s_b, p_a, p_b, acc_ref, m_ref, l_ref, lo_ref, len_ref, mc_ref, ratio_ref,
           send_kv, send_q, send_o, recv_kv, recv_q, recv_o, send_y, recv_y, send_r, recv_r, send_s, recv_s, own_sem):
    nz, ny = heads // XL, blocks // (XH * CORES)
    half = ny * CORES
    hc, bc = lax.axis_index("head"), lax.axis_index("blk")
    z, xl = lax.div(hc, XL), lax.rem(hc, XL)
    xh, r = lax.div(bc, half), lax.rem(bc, half)
    y, c = lax.div(r, CORES), lax.rem(r, CORES)
    seqs, tok = kc_hbm.shape[0], kc_hbm.shape[1]
    TQ = XL * XH * tok
    CK = XH * half * tok
    SB = 2 * CORES * tok
    period = half * tok
    scale = math.log2(math.e) / math.sqrt(float(HD))

    loads = [pltpu.make_async_copy(ref, codes.at[i], own_sem.at[3 + i]) for i, ref in enumerate((kc_hbm, vc_hbm))]
    for cp in loads:
        cp.start()

    def dev(z_, xl_, xh_, y_, c_):
        return (z_ * XL + xl_, xh_ * half + y_ * CORES + c_)

    up, down, far = lax.rem(y + 1, ny), lax.rem(y + ny - 1, ny), lax.rem(y + 2, ny)
    order = [(k + 1) // 2 if k % 2 else (nz - k // 2) % nz for k in range(nz)]
    offsets = [(dl, dh) for dl in range(XL) for dh in range(XH)]
    partners = [(dz, dl, dh) for dz in order for dl, dh in offsets if (dz, dl, dh) != (0, 0, 0)]
    barrier = pltpu.get_barrier_semaphore()
    targets = [dev(lax.rem(z + dz, nz), xl ^ dl, xh ^ dh, y, c) for dz, dl, dh in partners]
    targets += [dev(z, xl, xh, up, c), dev(z, xl, xh, down, c), dev(z, xl, xh, y, 1 - c)]
    for t in targets:
        pl.semaphore_signal(barrier, inc=1, device_id=t, device_id_type=MESH)

    had = hadamard_matrix()
    head_of_lane = lax.broadcasted_iota(jnp.int32, (heads, heads * HD), 1) // HD
    pick = jnp.where(head_of_lane == lax.broadcasted_iota(jnp.int32, (heads, heads * HD), 0), 1.0, 0.0).astype(jnp.bfloat16)
    for which, scales in enumerate((ks_ref, vs_ref)):
        for n in range(seqs):
            wide[which, n] = lax.dot_general(
                scales[n], pick, (((0,), (0,)), ((), ())), preferred_element_type=jnp.float32) * HD ** (-0.5)
        loads[which].wait()

    def dequantize(dz):
        for which in range(2):
            for l in range(XL):
                h = lax.rem(z + nz - dz, nz) * XL + l
                cols = pl.ds(pl.multiple_of(h * HD, HD), HD)
                mixed = jnp.dot(codes[which, :, :, cols].reshape(seqs * tok, HD), had, preferred_element_type=jnp.float32)
                for n in range(seqs):
                    stage[n, h, which] = (mixed[n * tok:(n + 1) * tok] * wide[which, n, :, cols]).astype(jnp.bfloat16)

    dequantize(0)
    pl.semaphore_wait(barrier, len(targets))

    own_kv = pltpu.make_async_copy(stage.at[xh, hc], kv.at[hc, xh, y, c], own_sem.at[0])
    own_kv.start()
    own_q = pltpu.make_async_copy(
        q_hbm.at[xh, :, pl.ds(pl.multiple_of(hc * HD, HD), HD)], qv.at[hc, xh], own_sem.at[1])
    own_q.start()

    def exchange(i, src, dst, send, recv):
        dz, dl, dh = partners[i]
        tz, tl, th = lax.rem(z + nz - dz, nz), xl ^ dl, xh ^ dh
        return pltpu.make_async_remote_copy(
            src_ref=src(tz * XL + tl, th), dst_ref=dst, send_sem=send.at[i], recv_sem=recv.at[i],
            device_id=dev(tz, tl, th, y, c), device_id_type=MESH)

    count = len(partners)
    kv_copies = [exchange(i, lambda h, n: stage.at[n, h], kv.at[hc, xh, y, c], send_kv, recv_kv) for i in range(count)]
    q_copies = [exchange(i, lambda h, n: q_hbm.at[n, :, pl.ds(pl.multiple_of(h * HD, HD), HD)], qv.at[hc, xh],
                         send_q, recv_q) for i in range(count)]

    def of_plane(copies, k):
        return [cp for p, cp in zip(partners, copies) if p[0] == order[k]]

    def part(k, ya, ca):
        return kv.at[pl.ds(lax.rem(z + order[k], nz) * XL, XL), :, ya, ca]

    def y_copy(k, way, incoming=False):
        ref = part(k, (down if way == 0 else up) if incoming else y, c)
        return pltpu.make_async_remote_copy(
            src_ref=ref, dst_ref=ref, send_sem=send_y.at[way, k], recv_sem=recv_y.at[way, k],
            device_id=dev(z, xl, xh, up if way == 0 else down, c), device_id_type=MESH)

    def relay_copy(k, way, incoming=False):
        ref = kv.at[lax.rem(z + order[k], nz) * XL + way, :, far if incoming else (down if way == 0 else up), c]
        return pltpu.make_async_remote_copy(
            src_ref=ref, dst_ref=ref, send_sem=send_r.at[way, k], recv_sem=recv_r.at[way, k],
            device_id=dev(z, xl, xh, up if way == 0 else down, c), device_id_type=MESH)

    def sib_copy(k, j, ca):
        ref = part(k, (y, down, up, far)[j], ca)
        return pltpu.make_async_remote_copy(
            src_ref=ref, dst_ref=ref, send_sem=send_s.at[j, k], recv_sem=recv_s.at[j, k],
            device_id=dev(z, xl, xh, y, 1 - c), device_id_type=MESH)

    def send_keys(k):
        for cp in of_plane(kv_copies, k):
            cp.start()

    def send_queries():
        for cp in q_copies:
            cp.start()

    def queries():
        for cp in q_copies:
            cp.wait_recv()
        own_q.wait()

    def arrived(k):
        for cp in of_plane(kv_copies, k):
            cp.wait_recv()
        if k == 0:
            own_kv.wait()
        y_copy(k, 0).start()
        y_copy(k, 1).start()
        sib_copy(k, 0, c).start()

    def passed(k):
        for way in range(2):
            y_copy(k, way, True).wait_recv()
            relay_copy(k, way).start()
            sib_copy(k, 1 + way, c).start()

    def rounded(k):
        relay_copy(k, 0, True).wait_recv()
        relay_copy(k, 1, True).wait_recv()
        sib_copy(k, 3, c).start()

    def whole(k):
        for j in range(4):
            sib_copy(k, j, 1 - c).wait_recv()

    for k in range(nz):
        if k:
            dequantize(order[k])
        if k == 3:
            send_queries()
        if k < 5:
            send_keys(k)

    ends = []
    for i in range(doc_ref.shape[1]):
        one = jnp.where(xh == 0, doc_ref[0, i], doc_ref[seqs - 1, i])
        ends.append(one + (ends[-1] if ends else 0))
    lane = lax.broadcasted_iota(jnp.int32, (8, TQ), 1)
    sub = lax.broadcasted_iota(jnp.int32, (8, TQ), 0)

    def prepare(t, _):
        qpos = t * (XL * XH * period) + r * tok + lax.div(lane, tok) * period + lax.rem(lane, tok)
        ds = jnp.zeros((8, TQ), jnp.int32)
        for e in ends:
            ds = jnp.maximum(ds, jnp.where(qpos >= e, e, 0))
        lo_ref[t] = sub - ds + LEAST
        len_ref[t] = qpos - ds + LEAST
        m_ref[t] = jnp.full((8, TQ), NEG, jnp.float32)
        l_ref[t] = jnp.zeros((8, TQ), jnp.float32)
        acc_ref[t] = jnp.zeros((HD, TQ), jnp.float32)
        return 0

    lax.fori_loop(0, nz + 1, prepare, 0)
    for i in range(2):
        mc_ref[i] = jnp.zeros((8, TQ), jnp.float32)
        ratio_ref[i] = jnp.zeros((8, TQ), jnp.float32)
    for ref in (s_a, s_b, p_a, p_b):
        ref[...] = jnp.zeros_like(ref)

    bufs = ((s_a, p_a), (s_b, p_b))
    pieces = CK // SB

    def chunk(zk, h, which, b):
        ys = SB // (CORES * tok)
        return kv[zk * XL + h, b * ys // ny, pl.ds(b * ys % ny, ys), :, which].reshape(SB, HD)

    def scores(t, zk, h):
        s_w = bufs[h][0]
        q = qv[pl.ds(t * XL, XL)].reshape(TQ, HD)
        lo, ln = lo_ref[t] + (zk * XL + h) * CK, len_ref[t]
        old = m_ref[t]
        ms = [old, old]

        def piece(b):
            s = lax.dot_general(chunk(zk, h, 0, b), q, (((1,), (1,)), ((), ())), preferred_element_type=jnp.float32)
            for i in range(SB // 8):
                si = jnp.where(lo + (b * SB + i * 8) <= ln, s[i * 8:(i + 1) * 8], NEG)
                s_w[pl.ds(b * SB + i * 8, 8), :] = si
                ms[i % 2] = jnp.maximum(ms[i % 2], si)

        def finish():
            new = jnp.broadcast_to(jnp.max(jnp.maximum(ms[0], ms[1]), axis=0, keepdims=True), (8, TQ))
            m_ref[t] = new
            mc_ref[h] = new * scale
            ratio_ref[h] = jnp.exp2((old - new) * scale)

        return piece, finish

    def weights(t, h):
        s_r, p_w = bufs[h]
        mc = mc_ref[h]
        ls = [l_ref[t] * ratio_ref[h], jnp.zeros((8, TQ), jnp.float32)]

        def piece(b):
            prev = None
            for i in range(SB // 8):
                p = jnp.exp2(s_r[pl.ds(b * SB + i * 8, 8), :] * scale - mc)
                ls[i % 2] = ls[i % 2] + p
                if i % 2:
                    p_w[pl.ds(b * SB + (i - 1) * 8, 16), :] = jnp.concatenate([prev, p], 0).astype(jnp.bfloat16)
                prev = p

        def finish():
            l_ref[t] = ls[0] + ls[1]

        return piece, finish

    def products(t, zk, h):
        p_r = bufs[h][1]
        acc = [(acc_ref[t].reshape(HD // 8, 8, TQ) * ratio_ref[h][None]).reshape(HD, TQ)]

        def piece(b):
            if b % 2:
                v = jnp.concatenate([chunk(zk, h, 1, b - 1), chunk(zk, h, 1, b)], 0)
                acc[0] = acc[0] + lax.dot_general(
                    v, p_r[pl.ds((b - 1) * SB, 2 * SB), :], (((0,), (0,)), ((), ())), preferred_element_type=jnp.float32)

        def finish():
            acc_ref[t] = acc[0]

        return piece, finish

    def run(parts):
        for b in range(pieces):
            for piece, _ in parts:
                piece(b)
        for _, finish in parts:
            finish()

    def pair_step(t, zk, t_old, zk_old):
        run([products(t_old, zk_old, 0), weights(t_old, 1), scores(t, zk, 0)])
        run([products(t_old, zk_old, 1), weights(t, 0), scores(t, zk, 1)])

    def plane_at(k):
        odd = lax.rem(k, 2)
        return lax.rem(z + odd * lax.div(k + 1, 2) + (1 - odd) * (nz - lax.div(k, 2)), nz)

    todo = {
        (0, 0): [(arrived, 0), (arrived, 1), (arrived, 2), (passed, 0), (passed, 1), (rounded, 0), (passed, 2), (whole, 0), (rounded, 1),
                 (queries,)],
        (0, 1): [(whole, 1), (rounded, 2), (send_keys, 5), (send_keys, 6)],
        (0, 2): [(arrived, 3)],
        (1, 0): [(arrived, 4), (whole, 2), (send_keys, 7)],
        (1, 1): [(passed, 3)],
        (2, 0): [(passed, 4)],
        (2, 1): [(rounded, 3)],
        (2, 2): [(arrived, 5)],
        (3, 0): [(rounded, 4), (whole, 3), (arrived, 6)],
        (3, 1): [(passed, 5)],
        (3, 2): [(arrived, 7)],
        (4, 0): [(whole, 4), (passed, 6)],
        (4, 1): [(rounded, 5)],
        (4, 2): [(passed, 7)],
        (5, 0): [(whole, 5), (rounded, 6)],
        (5, 2): [(rounded, 7)],
        (6, 0): [(whole, 6)],
    }

    def tiles_of(zk):
        return nz // 2 + 1 - (zk - nz // 2 + 1) * lax.div(zk, nz // 2)

    def with_plane(n, carry):
        zk = plane_at(n)
        tiles = tiles_of(zk)

        def with_part(u, carry):
            for (at_n, at_u), steps in todo.items():
                @pl.when(3 * n + u == 3 * at_n + at_u)
                def _(steps=steps):
                    for do, *k in steps:
                        do(*k)

            def with_tile(b, carry):
                t_old, zk_old = carry
                pair_step(zk + b, zk, t_old, zk_old)
                return zk + b, zk

            return lax.fori_loop(lax.div(u * tiles + 2, 3), lax.div((u + 1) * tiles + 2, 3), with_tile, carry)

        return lax.fori_loop(0, 3, with_part, carry)

    t_old, zk_old = lax.fori_loop(0, nz - 1, with_plane, (jnp.int32(nz), z))

    def o_copy(dz, dl, dh, t):
        i = dz * (XL * XH) + dl * XH + dh
        return pltpu.make_async_remote_copy(
            src_ref=ov.at[t * XL + (xl ^ dl), xh ^ dh],
            dst_ref=out_hbm.at[xh, :, pl.ds(pl.multiple_of(hc * HD, HD), HD)],
            send_sem=send_o.at[i], recv_sem=recv_o.at[i],
            device_id=dev(t, xl ^ dl, xh ^ dh, y, c), device_id_type=MESH)

    own_o = pltpu.make_async_copy(
        ov.at[hc, xh], out_hbm.at[xh, :, pl.ds(pl.multiple_of(hc * HD, HD), HD)], own_sem.at[2])

    def close(t):
        total = jnp.sum(l_ref[t], axis=0, keepdims=True)
        o = (acc_ref[t] / total).T
        ov[pl.ds(t * XL, XL)] = o.astype(jnp.bfloat16).reshape(XL, XH, tok, HD)
        dz = lax.rem(z + nz - t, nz)
        for dl, dh in offsets:
            if (dl, dh) == (0, 0):
                @pl.when(t == z)
                def _():
                    own_o.start()

                @pl.when(t != z)
                def _():
                    o_copy(dz, 0, 0, t).start()
            else:
                o_copy(dz, dl, dh, t).start()

    def close_at(t, carry):
        close(t)
        return carry

    whole(nz - 1)
    last = plane_at(nz - 1)
    tiles = tiles_of(last)
    pair_step(last, last, t_old, zk_old)
    lax.fori_loop(0, last, close_at, 0)
    lax.fori_loop(last + tiles, nz, close_at, 0)

    def last_tile(b, carry):
        pair_step(last + b, last, last + b - 1, last)
        close(last + b - 1)
        return carry

    lax.fori_loop(1, tiles, last_tile, 0)
    end = last + tiles - 1
    run([products(end, last, 0), weights(end, 1)])
    run([products(end, last, 1)])
    close(end)
    own_o.wait()
    for dz in range(nz):
        for dl, dh in offsets:
            if (dz, dl, dh) != (0, 0, 0):
                o_copy(dz, dl, dh, lax.rem(z + nz - dz, nz)).wait()
    for cp in kv_copies + q_copies:
        cp.wait_send()
    for k in range(nz):
        for way in range(2):
            y_copy(k, way).wait_send()
            relay_copy(k, way).wait_send()
        for j in range(4):
            sib_copy(k, j, c).wait_send()


def body(heads, blocks, queries, key_codes, key_scales, value_codes, value_scales, doc_lengths):
    seqs, tok, width = queries.shape
    nz, ny = heads // XL, blocks // (XH * CORES)
    n = heads * XH - 1
    tq, ck = XL * XH * tok, blocks * tok
    dma = pltpu.SemaphoreType.DMA
    vm, hbm = pl.BlockSpec(memory_space=pltpu.VMEM), pl.BlockSpec(memory_space=pl.ANY)
    per_tile = lambda count, dt: pltpu.VMEM((count, 8, tq), dt)
    return pl.pallas_call(
        functools.partial(kernel, heads, blocks),
        out_shape=pltpu.VMEM(queries.shape, jnp.bfloat16),
        in_specs=[pl.BlockSpec(memory_space=pltpu.SMEM), hbm, hbm, vm, hbm, vm],
        out_specs=vm,
        scratch_shapes=[
            pltpu.VMEM((2, seqs, tok, width), jnp.bfloat16),
            pltpu.VMEM((2, seqs, tok, width), jnp.float32),
            pltpu.VMEM((seqs, heads, 2, tok, HD), jnp.bfloat16),
            pltpu.VMEM((heads, XH, ny, CORES, 2, tok, HD), jnp.bfloat16),
            pltpu.VMEM((heads, XH, tok, HD), jnp.bfloat16),
            pltpu.VMEM((heads, XH, tok, HD), jnp.bfloat16),
            pltpu.VMEM((ck, tq), jnp.float32),
            pltpu.VMEM((ck, tq), jnp.float32),
            pltpu.VMEM((ck, tq), jnp.bfloat16),
            pltpu.VMEM((ck, tq), jnp.bfloat16),
            pltpu.VMEM((nz + 1, HD, tq), jnp.float32),
            per_tile(nz + 1, jnp.float32), per_tile(nz + 1, jnp.float32),
            per_tile(nz + 1, jnp.int32), per_tile(nz + 1, jnp.int32),
            per_tile(2, jnp.float32), per_tile(2, jnp.float32),
            dma((n,)), dma((n,)), dma((n + 1,)), dma((n,)), dma((n,)), dma((n + 1,)),
            dma((2, nz)), dma((2, nz)), dma((2, nz)), dma((2, nz)),
            dma((4, nz)), dma((4, nz)), dma((5,)),
        ],
        compiler_params=pltpu.CompilerParams(
            collective_id=0, has_side_effects=True, vmem_limit_bytes=VMEM_ASK),
    )(doc_lengths, queries, key_codes, jnp.transpose(key_scales, (0, 2, 1)),
      value_codes, jnp.transpose(value_scales, (0, 2, 1)))


def solution(mesh):
    rows = P(None, ("head", "blk"), None)
    return jax.shard_map(
        functools.partial(body, mesh.shape["head"], mesh.shape["blk"]),
        mesh=mesh,
        in_specs=(rows, rows, rows, rows, rows, P()),
        out_specs=rows,
        check_vma=False,
    )
```

profile of v0, /device:TPU:64, one launch (start us, length us, event | category | flops | bytes accessed | tf_op | source)
XLA Modules:
  0.0 90.8 jit_solution(259576834559177450)
XLA Ops:
  0.0 90.0 %shard_map.64 = bf16[2,64,2048]{2,1,0:T(8,128)(2,1)S(1)} custom-call(s32[2,8]{1,0:T(2,128)} %doc_ref.1, bf16[2,64,2048]{2,1,0:T(8,128)(2,1)} %q_hbm.1, bf16[2,64,2048]{2,1,0:T(8,128)(2,1)} %kc_hbm.1, bf16[2,16,64]{2,1,0:T(8,128)(2,1)} %bitcast.2, bf16[2,64,2048]{2,1,0:T(8,128)(2,1)} %vc_hbm.1, bf16[2,16,64]{2,1,0:T(8,128)(2,1)} %bitcast.3), custom_call_target="tpu_custom_call" | custom-call | tf_op jit(solution)/shard_map/pallas_call | solution.py:390
  90.0 0.8 copy.8
where the time goes:
time: 90.9 us; the launch traced here: 90.8 us
  Pallas kernels  90 us (99%)
    pallas_call x1, Pallas kernels, body(): pl.pallas_call(functools.partial(kernel, heads, blocks), out_shape=pltpu....  90 us

commit v1 on v0

--- a/solution.py
+++ b/solution.py
@@ -138,15 +138,15 @@
             cp.wait_recv()
         if k == 0:
             own_kv.wait()
+        sib_copy(k, 0, c).start()
         y_copy(k, 0).start()
         y_copy(k, 1).start()
-        sib_copy(k, 0, c).start()
 
     def passed(k):
         for way in range(2):
             y_copy(k, way, True).wait_recv()
+            sib_copy(k, 1 + way, c).start()
             relay_copy(k, way).start()
-            sib_copy(k, 1 + way, c).start()
 
     def rounded(k):
         relay_copy(k, 0, True).wait_recv()
@@ -198,17 +198,20 @@
         ys = SB // (CORES * tok)
         return kv[zk * XL + h, b * ys // ny, pl.ds(b * ys % ny, ys), :, which].reshape(SB, HD)
 
-    def scores(t, zk, h):
+    def scores(t, zk, h, own):
         s_w = bufs[h][0]
         q = qv[pl.ds(t * XL, XL)].reshape(TQ, HD)
         lo, ln = lo_ref[t] + (zk * XL + h) * CK, len_ref[t]
+        past = lo + LEAST
         old = m_ref[t]
         ms = [old, old]
 
         def piece(b):
             s = lax.dot_general(chunk(zk, h, 0, b), q, (((1,), (1,)), ((), ())), preferred_element_type=jnp.float32)
             for i in range(SB // 8):
-                si = jnp.where(lo + (b * SB + i * 8) <= ln, s[i * 8:(i + 1) * 8], NEG)
+                at = b * SB + i * 8
+                seen = lo + at <= ln if own else past >= -at
+                si = jnp.where(seen, s[i * 8:(i + 1) * 8], NEG)
                 s_w[pl.ds(b * SB + i * 8, 8), :] = si
                 ms[i % 2] = jnp.maximum(ms[i % 2], si)
 
@@ -261,9 +264,9 @@
         for _, finish in parts:
             finish()
 
-    def pair_step(t, zk, t_old, zk_old):
-        run([products(t_old, zk_old, 0), weights(t_old, 1), scores(t, zk, 0)])
-        run([products(t_old, zk_old, 1), weights(t, 0), scores(t, zk, 1)])
+    def pair_step(own, t, zk, t_old, zk_old):
+        run([products(t_old, zk_old, 0), weights(t_old, 1), scores(t, zk, 0, own)])
+        run([products(t_old, zk_old, 1), weights(t, 0), scores(t, zk, 1, own)])
 
     def plane_at(k):
         odd = lax.rem(k, 2)
@@ -304,12 +307,15 @@
                     for do, *k in steps:
                         do(*k)
 
-            def with_tile(b, carry):
+            def with_tile(own, b, carry):
                 t_old, zk_old = carry
-                pair_step(zk + b, zk, t_old, zk_old)
+                pair_step(own, zk + b, zk, t_old, zk_old)
                 return zk + b, zk
 
-            return lax.fori_loop(lax.div(u * tiles + 2, 3), lax.div((u + 1) * tiles + 2, 3), with_tile, carry)
+            low = lax.div(u * tiles + 2, 3)
+            high = low + lax.div(2 - u, 2)
+            carry = lax.fori_loop(low, high, functools.partial(with_tile, True), carry)
+            return lax.fori_loop(high, lax.div((u + 1) * tiles + 2, 3), functools.partial(with_tile, False), carry)
 
         return lax.fori_loop(0, 3, with_part, carry)
 
@@ -350,12 +356,12 @@
     whole(nz - 1)
     last = plane_at(nz - 1)
     tiles = tiles_of(last)
-    pair_step(last, last, t_old, zk_old)
+    pair_step(True, last, last, t_old, zk_old)
     lax.fori_loop(0, last, close_at, 0)
     lax.fori_loop(last + tiles, nz, close_at, 0)
 
     def last_tile(b, carry):
-        pair_step(last + b, last, last + b - 1, last)
+        pair_step(False, last + b, last, last + b - 1, last)
         close(last + b - 1)
         return carry
 

time: 90.9 us -> 90.1 us (level)
  no operation moved by 1% of the time
where the time goes in v1:
time: 90.1 us; the launch traced here: 89.9 us
  Pallas kernels  89.1 us (99%)
    pallas_call x1, Pallas kernels, body(): pl.pallas_call(functools.partial(kernel, heads, blocks), out_shape=pltpu....  89.1 us

profile of v1, /device:TPU:64, one launch (start us, length us, event | category | flops | bytes accessed | tf_op | source)
XLA Modules:
  0.0 89.9 jit_solution(9859046839053973446)
XLA Ops:
  0.0 89.1 %shard_map.64 = bf16[2,64,2048]{2,1,0:T(8,128)(2,1)S(1)} custom-call(s32[2,8]{1,0:T(2,128)} %doc_ref.1, bf16[2,64,2048]{2,1,0:T(8,128)(2,1)} %q_hbm.1, bf16[2,64,2048]{2,1,0:T(8,128)(2,1)} %kc_hbm.1, bf16[2,16,64]{2,1,0:T(8,128)(2,1)} %bitcast.2, bf16[2,64,2048]{2,1,0:T(8,128)(2,1)} %vc_hbm.1, bf16[2,16,64]{2,1,0:T(8,128)(2,1)} %bitcast.3), custom_call_target="tpu_custom_call" | custom-call | tf_op jit(solution)/shard_map/pallas_call | solution.py:396
  89.1 0.8 copy.8
